TPU v7x, 512 devices: a whole 4x4x16 slice. The times are simulated.
512 devices in a mesh: ctx: 32 (over z, core), inner: 16 (over y, x).
Axes of the slice: x: 4, y: 4, z: 16, core: 2. Of those that a mesh axis runs over, the one named last changes fastest.
Arguments:
- tokens: bfloat16 [65536, 2048], P(('ctx', 'inner')), may hold values from -6 to 6
- project_weight: bfloat16 [2048, 2, 4096], P('ctx', None, 'inner'), may hold values from -0.125 to 0.125
- state_weight: bfloat16 [2048, 2, 512], P('ctx', None, 'inner'), may hold values from -0.125 to 0.125
- step_weight: bfloat16 [2048, 64], P('ctx', 'inner'), may hold values from -0.125 to 0.125
- mixer_taps: float32 [5, 4096], P(None, 'inner'), may hold values from -2.5 to 2.5
- state_taps: float32 [5, 2, 512], replicated, may hold values from -2.5 to 2.5
- step_bias: float32 [64], P('inner'), may hold values from -4.6 to -2.3
- decay_log: float32 [64], P('inner'), may hold values from -13 to 0.5, as said below
- norm_gain: float32 [4096], replicated, may hold values from 0.1 to 1.9
Outputs:
- mixed_output: bfloat16 [65536, 4096], P(('ctx', 'inner'))
Inputs may be any that keep to these rules, and one draw needn't show every extreme that they name: `decay_log`: one value a head.
All inputs are finite; a program needn't handle non-finite values.
Results may differ from a plain program's by a relative error of at most 0.0075.
Values may be sent and summed in bfloat16 or wider, within the bound.
A program may use at most 64 MiB of HBM per device.

v0:
```python
import jax
import jax.numpy as jnp
from jax import lax
from jax.sharding import PartitionSpec as P

H = 64
P_SIZE = 64
N = 128
G = 4
CONV = 4
SPAN = 128
EPSILON = 1e-05


def passed_along(x, axis, by):
    count = lax.axis_size(axis)
    pairs = [(i, i + by) for i in range(count) if 0 <= i + by < count]
    return lax.ppermute(x, axis, pairs)


def entering(x, axis, join, neutral):
    place = lax.axis_index(axis)
    gathered = jax.tree.map(
        lambda a, kind: lax.all_gather(a.astype(kind), axis), x, (jnp.bfloat16, jnp.bfloat16)
    )
    state = jax.tree.map(lambda a, e: jnp.zeros_like(a) + jnp.asarray(e, a.dtype), x, neutral)

    def one(turn, state):
        return join(
            state,
            jax.tree.map(
                lambda a, own: lax.dynamic_index_in_dim(a, turn, 0, False).astype(own.dtype),
                gathered,
                x,
            ),
        )

    return lax.fori_loop(0, place, one, state)


def partner(value, axis, stride):
    mask = 2**stride
    pairs = [(source, source ^ mask) for source in range(lax.axis_size(axis))]
    return lax.ppermute(value, axis, pairs)


def conv_apply(taps, previous, current):
    extended = jnp.concatenate([previous, current], axis=0)
    length_rows = current.shape[0]
    mixed = jnp.broadcast_to(taps[CONV], current.shape)
    for offset in range(CONV):
        mixed = mixed + taps[offset] * extended[offset : offset + length_rows].astype(jnp.float32)
    return jax.nn.silu(mixed).astype(jnp.bfloat16)


def join_chain(earlier, later):
    return (earlier[0] + later[0], jnp.exp(later[0])[:, None, None] * earlier[1] + later[1])


def carry_block(state, inputs):
    decay_sum, added = inputs
    return (jnp.exp(decay_sum)[:, None, None] * state + added, state)


def pick_group(values, group):
    shaped = values.reshape(values.shape[:-1] + (N, G))
    return lax.dynamic_index_in_dim(shaped, group, shaped.ndim - 1, keepdims=False)


def on_device(
    tokens,
    project_weight,
    state_weight,
    step_weight,
    mixer_taps,
    state_taps,
    step_bias,
    decay_log,
    norm_gain,
):
    inner_id = lax.axis_index("inner")
    project_rows, state_rows, step_rows = (
        lax.all_gather(project_weight, "ctx", axis=0, tiled=True),
        lax.all_gather(state_weight, "ctx", axis=0, tiled=True),
        lax.all_gather(step_weight, "ctx", axis=0, tiled=True),
    )
    heads_here = step_weight.shape[1]
    width_here = project_weight.shape[2]
    model_width = project_rows.shape[0]
    group = inner_id * heads_here // (H // G)
    full_cols = lax.all_gather(state_rows, "inner", axis=2, tiled=True)
    slice_cols = N
    state_cols = pick_group(full_cols, group)
    state_conv = pick_group(state_taps, group)
    joined = jnp.concatenate(
        [
            project_rows.reshape(model_width, 2 * width_here),
            state_cols.reshape(model_width, 2 * slice_cols),
            step_rows,
        ],
        axis=1,
    )
    projected = jnp.dot(
        lax.all_gather(tokens, "inner", axis=0, tiled=True),
        joined,
        preferred_element_type=jnp.float32,
    ).astype(jnp.bfloat16)
    rows_total = projected.shape[0]
    gate_values = projected[:, :width_here]
    x_pre = projected[:, width_here : 2 * width_here]
    state_pre = projected[:, 2 * width_here : 2 * width_here + 2 * slice_cols].reshape(
        rows_total, 2, slice_cols
    )
    step_raw = projected[:, 2 * width_here + 2 * slice_cols :]
    edge_row = rows_total - (CONV - 1)
    prior_x, prior_state = passed_along((x_pre[edge_row:], state_pre[edge_row:]), "ctx", 1)
    x_vals = conv_apply(mixer_taps, prior_x, x_pre)
    state_vals = conv_apply(state_conv, prior_state, state_pre)
    blocks = rows_total // SPAN
    b_blocks = state_vals[:, 0].reshape(blocks, SPAN, N)
    c_blocks = state_vals[:, 1].reshape(blocks, SPAN, N)
    step_size = jax.nn.softplus(step_raw.astype(jnp.float32) + step_bias)
    step_heads = step_size.T.reshape(heads_here, blocks, SPAN)
    cumul = jnp.cumsum(step_heads * (-jnp.exp(decay_log))[:, None, None], axis=2)
    scores = jnp.einsum("ctn,csn->cts", c_blocks, b_blocks, preferred_element_type=jnp.float32)
    lower = jnp.tril(jnp.ones((SPAN, SPAN), dtype=bool))
    spacing = jnp.where(lower, cumul[..., :, None] - cumul[..., None, :], -jnp.inf)
    mixing = (scores[None] * jnp.exp(spacing) * step_heads[:, :, None, :]).astype(jnp.bfloat16)
    x_blocks = x_vals.reshape(blocks, SPAN, heads_here, P_SIZE)
    diagonal = jnp.einsum("hcts,cshp->cthp", mixing, x_blocks, preferred_element_type=jnp.float32)
    ending = cumul[:, :, -1]
    to_end = jnp.exp(ending[..., None] - cumul) * step_heads
    weighted_b = (b_blocks.astype(jnp.float32)[None] * to_end[..., None]).astype(jnp.bfloat16)
    fresh = jnp.einsum("hcsn,cshp->chnp", weighted_b, x_blocks, preferred_element_type=jnp.float32)
    empty_state = jnp.zeros((heads_here, N, P_SIZE), jnp.float32)
    block_state, local_in = lax.scan(carry_block, empty_state, (ending.T, fresh))
    block_log = jnp.sum(ending, axis=1)
    before_log = (jnp.cumsum(ending, axis=1) - ending).T
    _, prior_block = entering(
        (block_log, block_state), "ctx", join_chain, (jnp.zeros_like(block_log), empty_state)
    )
    state_in = local_in + jnp.exp(before_log)[:, :, None, None] * prior_block[None]
    c_scaled = (c_blocks.astype(jnp.float32)[None] * jnp.exp(cumul)[..., None]).astype(jnp.bfloat16)
    state_high = state_in.astype(jnp.bfloat16)
    state_low = (state_in - state_high.astype(jnp.float32)).astype(jnp.bfloat16)
    offdiag = jnp.einsum(
        "hctn,chnp->cthp", c_scaled, state_high, preferred_element_type=jnp.float32
    )
    offdiag = offdiag + jnp.einsum(
        "hctn,chnp->cthp", c_scaled, state_low, preferred_element_type=jnp.float32
    )
    outputs = (diagonal + offdiag).reshape(rows_total, width_here)
    gated = (outputs * jax.nn.silu(gate_values.astype(jnp.float32))).astype(jnp.bfloat16)
    gated_wide = gated.astype(jnp.float32)
    squares = jnp.sum(gated_wide * gated_wide, axis=1)
    group_devices = H // G // heads_here
    for bit in range(group_devices.bit_length() - 1):
        squares = squares + partner(squares, "inner", bit)
    power = squares[:, None] / (H * P_SIZE // G)
    gain_here = lax.dynamic_slice_in_dim(norm_gain, inner_id * width_here, width_here, 0)
    normed = (gated_wide * lax.rsqrt(power + EPSILON) * gain_here).astype(jnp.bfloat16)
    result = lax.all_to_all(normed, "inner", split_axis=0, concat_axis=1, tiled=True)
    return result


def solution(mesh):
    placed = (
        P(("ctx", "inner"), None),
        P("ctx", None, "inner"),
        P("ctx", None, "inner"),
        P("ctx", "inner"),
        P(None, "inner"),
        P(),
        P("inner"),
        P("inner"),
        P(),
    )
    return jax.shard_map(
        on_device, mesh=mesh, in_specs=placed, out_specs=P(("ctx", "inner"), None), check_vma=False
    )
```

profile of v0, /device:TPU:480, one launch (start us, length us, event | category | flops | bytes accessed | tf_op | source)
XLA Modules:
  0.0 455.8 jit_solution(17512234280697024061)
XLA Ops:
  8.1 30.7 %all_gather.26 = bf16[2048,2,32]{2,1,0:T(2,128)(2,1)S(1)} all-gather(bf16[64,2,32]{2,1,0:T(2,128)(2,1)S(1)} %copy.91), channel_id=1, replica_groups=mesh['ctx'=32,'inner'=16] {'ctx'}, dimensions={0}, use_global_device_ids=true | all-gather | bytes 270336 | tf_op jit(solution)/shard_map/all_gather | solution.py:84
  38.8 1.8 copy.92
  41.4 29.1 %all-gather.2 = bf16[32,64,4]{1,2,0:T(4,128)(2,1)S(1)} all-gather(bf16[1,64,4]{1,2,0:T(4,128)(2,1)S(1)} %bitcast.102), channel_id=1, replica_groups=mesh['ctx'=32,'inner'=16] {'ctx'}, dimensions={0}, use_global_device_ids=true | all-gather | bytes 16896 | tf_op jit(solution)/shard_map/all_gather | solution.py:85
  70.5 1.1 copy.119
  72.8 6.1 %all-gather.8.cloned.1.call-done = bf16[2048,2,256]{2,1,0:T(2,128)(2,1)} async-done(((bf16[64,2,256]{2,1,0:T(2,128)(2,1)}), bf16[2048,2,256]{2,1,0:T(2,128)(2,1)}) %all-gather.8.cloned.1.call-update) | async-done | bytes 2097168 | tf_op jit(solution)/shard_map/all_gather | solution.py:83
  78.9 2.0 copy.123
  81.0 66.3 %all-gather.10.cloned.1.call-done = bf16[2048,2,512]{0,1,2:T(2,128)(2,1)} async-done(((bf16[2048,2,32]{0,1,2:T(2,128)(2,1)}), bf16[2048,2,512]{0,1,2:T(2,128)(2,1)}) %all-gather.10.cloned.1.call-update) | async-done | bytes 4194320 | tf_op jit(solution)/shard_map/all_gather | solution.py:91
  147.3 1.9 constant_dynamic-slice_fusion.2
  149.6 1.3 copy.95
  150.9 85.3 %all-gather.12.cloned.1.call-done = bf16[2048,2048]{1,0:T(8,128)(2,1)} async-done(((bf16[128,2048]{1,0:T(8,128)(2,1)}), bf16[2048,2048]{1,0:T(8,128)(2,1)}) %all-gather.12.cloned.1.call-update) | async-done | bytes 8388624 | tf_op jit(solution)/shard_map/all_gather | solution.py:104
  236.1 10.8 %fusion.12 = bf16[2048,772]{0,1:T(8,128)(2,1)S(1)} fusion(bf16[2048,2048]{1,0:T(8,128)(2,1)} %all-gather.12.cloned.1.call-done, bf16[2048,4]{1,0:T(8,128)(2,1)} %bitcast.92, bf16[2048,256]{1,0:T(8,128)(2,1)} %copy.95, bf16[2048,512]{1,0:T(8,128)(2,1)S(1)} %bitcast.91), kind=kOutput, calls=%fused_computation.21 | convolution fusion | flops 6487072768 | bytes 14712832 | tf_op jit(solution)/shard_map/dot_general | solution.py:103
  247.2 1.4 copy-done.1
  248.8 1.1 reduce_window_sum.22
  250.2 1.9 collective-permute-start
  252.2 2.1 collective-permute-start.1
  254.4 1.4 collective-permute-done
  255.7 2.2 fusion.51
  258.2 2.2 multiply_convert_fusion.7
  260.8 3.9 fusion.26
  264.7 28.8 %while.26 = (s32[]{:T(128)}, f32[4,128,64]{2,1,0:T(8,128)S(1)}, f32[16,4,128,64]{3,2,1,0:T(8,128)}, f32[16,4]{1,0:T(8,128)S(1)}, f32[16,4,128,64]{3,2,1,0:T(8,128)}, /*index=5*/s32[]{:T(128)}, s32[]{:T(128)}) while((s32[]{:T(128)}, f32[4,128,64]{2,1,0:T(8,128)S(1)}, f32[16,4,128,64]{3,2,1,0:T(8,128)}, f32[16,4]{1,0:T(8,128)S(1)}, ...), condition=%wide.region_2.3_spmd.clone, body=%wide.region_1.2_spmd.clone.sunk | while | flops 131075 | bytes 787088 | solution.py:136
  265.5 1.0 bitcast_add_fusion.2
  267.3 1.0 bitcast_add_fusion.2
  269.1 1.0 bitcast_add_fusion.2
  270.9 1.0 bitcast_add_fusion.2
  272.7 1.0 bitcast_add_fusion.2
  274.5 1.0 bitcast_add_fusion.2
  276.3 1.0 bitcast_add_fusion.2
  278.1 1.0 bitcast_add_fusion.2
  279.9 1.0 bitcast_add_fusion.2
  281.8 1.0 bitcast_add_fusion.2
  283.6 1.0 bitcast_add_fusion.2
  285.4 1.0 bitcast_add_fusion.2
  287.2 1.0 bitcast_add_fusion.2
  294.4 1.3 dynamic-slice
  296.8 42.4 %all-reduce = bf16[128]{0:T(256)(128)(2,1)S(1)} all-reduce(bf16[128]{0:T(256)(128)(2,1)S(1)} %dynamic-update-slice), channel_id=2, replica_groups=mesh['ctx'=32,'inner'=16] {'ctx'}, use_global_device_ids=true, to_apply=%add | all-reduce | flops 128 | bytes 512
  340.3 3.3 fusion.18
  343.6 22.2 %all-gather.14.cloned.1.call-done = bf16[128,128,64]{1,2,0:T(8,128)(2,1)} async-done(((bf16[4,128,64]{1,2,0:T(8,128)(2,1)}), bf16[128,128,64]{1,2,0:T(8,128)(2,1)}) %all-gather.14.cloned.1.call-update) | async-done | bytes 2097168 | tf_op jit(solution)/shard_map/all_gather | solution.py:24
  365.8 34.4 %while.25 = (s32[]{:T(128)}, f32[4,128,64]{2,1,0:T(8,128)S(1)}, s32[]{:T(128)}, bf16[32,4]{1,0:T(8,128)(2,1)S(1)}, bf16[32,4,128,64]{2,3,1,0:T(8,128)(2,1)}, /*index=5*/s32[]{:T(128)}, s32[]{:T(128)}, s32[]{:T(128)}) while((s32[]{:T(128)}, f32[4,128,64]{2,1,0:T(8,128)S(1)}, s32[]{:T(128)}, bf16[32,4]{1,0:T(8,128)(2,1)S(1)}, ...), condition=%wide.region_6.7_spmd, body=%wide.region_5.6_spmd.sunk | while | flops 98313 | bytes 589991 | solution.py:38
  400.2 5.2 %fusion.15 = f32[16,4,64,128]{3,2,1,0:T(8,128)S(1)} fusion(f32[16,4,128,64]{3,2,1,0:T(8,128)} %get-tuple-element.77, f32[4,16,128]{2,0,1:T(4,128)S(1)} %copy.110, f32[16,128,128]{2,1,0:T(8,128)S(1)} %convert_element_type.135, f32[4,128,64]{2,1,0:T(8,128)S(1)} %get-tuple-element.79, f32[16,4]{1,0:T(8,128)S(1)} %copy.107), kind=kOutput, calls=%fused_computation.22 | convolution fusion | flops 139460608 | bytes 5406976 | tf_op jit(solution)/shard_map/hctn,chnp->cthp/dot_general | solution.py:149
  405.5 2.7 add_bitcast_fusion
  408.2 1.2 copy.113
  409.4 2.4 fusion.23
  411.8 3.4 collective-permute-start.2
  415.2 2.2 collective-permute-done.2
  417.4 4.9 %collective-permute-start.3 = (f32[2048]{0:T(1024)S(1)}, f32[2048]{0:T(1024)S(1)}, u32[]{:S(2)}, u32[]{:S(2)}) collective-permute-start(f32[2048]{0:T(1024)S(1)} %add.124), channel_id=1, source_target_pairs={{0,2},{1,3},{2,0},{3,1},{4,6},{5,7},{6,4},{7,5},{8,10},{9,11},{10,... | collective-permute-start | bytes 24584 | tf_op jit(solution)/shard_map/ppermute | solution.py:44
  423.0 1.4 collective-permute-done.3
  424.8 23.1 %all_to_all.19 = bf16[16,128,256]{1,2,0:T(8,128)(2,1)S(1)} all-to-all(bf16[16,128,256]{1,2,0:T(8,128)(2,1)S(1)} %copy_bitcast_fusion), channel_id=1, replica_groups=mesh['ctx'=32,'inner'=16] {'inner'}, dimensions={0} | all-to-all | bytes 2097152 | tf_op jit(solution)/shard_map/all_to_all | solution.py:162
  448.0 1.3 copy.115
  (217 shorter events, 56.9 us)
Async XLA Ops:
  6.5 34.9 %copy-start.5 = (bf16[64,4]{0,1:T(4,128)(2,1)S(1)}, bf16[64,4]{0,1:T(4,128)(2,1)}, u32[]{:S(2)}) copy-start(bf16[64,4]{0,1:T(4,128)(2,1)} %param.16) | copy-start | bytes 1540
  6.5 65.1 %copy-start.3 = (f32[5,2,512]{2,1,0:T(2,128)S(1)}, f32[5,2,512]{2,1,0:T(2,128)}, u32[]{:S(2)}) copy-start(f32[5,2,512]{2,1,0:T(2,128)} %param.18) | copy-start | bytes 61444
  6.5 72.4 %all-gather.8.cloned.1.call-start = ((), (), s32[]{:S(2)}) async-start(), calls=%async_computation.1 | async-start | bytes 2162688 | tf_op jit(solution)/shard_map/all_gather | solution.py:83
  7.3 140.0 %all-gather.10.cloned.1.call-start = ((), (), s32[]{:S(2)}) async-start(), calls=%async_computation.2 | async-start | bytes 4456448 | tf_op jit(solution)/shard_map/all_gather | solution.py:91
  38.8 34.0 %copy-start.7 = (f32[4]{0:T(128)S(1)}, f32[4]{0:T(128)}, u32[]{:S(2)}) copy-start(f32[4]{0:T(128)} %param.20) | copy-start | bytes 52
  38.8 34.0 %copy-start.4 = (f32[5,256]{1,0:T(8,128)S(1)}, f32[5,256]{1,0:T(8,128)}, u32[]{:S(2)}) copy-start(f32[5,256]{1,0:T(8,128)} %param.17) | copy-start | bytes 15364
  40.6 195.5 %all-gather.12.cloned.1.call-start = ((), (), s32[]{:S(2)}) async-start(), calls=%async_computation.3 | async-start | bytes 8912896 | tf_op jit(solution)/shard_map/all_gather | solution.py:104
  41.3 324.5 %all-gather.14.cloned.1.call-start = ((), (), s32[]{:S(2)}) async-start(), calls=%async_computation.4 | async-start | bytes 2162688 | tf_op jit(solution)/shard_map/all_gather | solution.py:24
  246.9 1.7 copy-start.1
  247.0 1.7 copy-start.6
  250.2 5.6 %collective-permute-start = (bf16[3,256]{0,1:T(8,128)(2,1)S(1)}, bf16[3,256]{0,1:T(8,128)(2,1)S(1)}, u32[]{:S(2)}, u32[]{:S(2)}) collective-permute-start(bf16[3,256]{0,1:T(8,128)(2,1)S(1)} %get-tuple-element.164), channel_id=1, source_target_pairs={{0,16},{16,32},{32,48},{48,64},{64,80},{80,96},{96,112},{112,128},... | collective-permute-start | bytes 4616 | tf_op jit(solution)/shard_map/ppermute | solution.py:18
  252.2 5.9 %collective-permute-start.1 = (bf16[3,2,128]{0,2,1:T(8,128)(2,1)S(1)}, bf16[3,2,128]{0,2,1:T(8,128)(2,1)S(1)}, u32[]{:S(2)}, u32[]{:S(2)}) collective-permute-start(bf16[3,2,128]{0,2,1:T(8,128)(2,1)S(1)} %bitcast.94), channel_id=1, source_target_pairs={{0,16},{16,32},{32,48},{48,64},{64,80},{80,96},{96,112},{112,128},... | collective-permute-start | bytes 4616 | tf_op jit(solution)/shard_map/ppermute | solution.py:18
  400.2 5.2 %copy-start = (f32[16,4,128,64]{3,2,1,0:T(8,128)S(1)}, f32[16,4,128,64]{3,2,1,0:T(8,128)}, u32[]{:S(2)}) copy-start(f32[16,4,128,64]{3,2,1,0:T(8,128)} %get-tuple-element.77) | copy-start | bytes 6291460
  400.2 5.2 %copy-start.2 = (f32[16,4,64,128]{3,2,1,0:T(8,128)S(1)}, f32[16,4,64,128]{3,2,1,0:T(8,128)}, u32[]{:S(2)}) copy-start(f32[16,4,64,128]{3,2,1,0:T(8,128)} %fusion.18) | copy-start | bytes 6291460
  411.8 5.5 %collective-permute-start.2 = (f32[2048]{0:T(1024)S(1)}, f32[2048]{0:T(1024)S(1)}, u32[]{:S(2)}, u32[]{:S(2)}) collective-permute-start(f32[2048]{0:T(1024)S(1)} %get-tuple-element.160), channel_id=1, source_target_pairs={{0,1},{1,0},{2,3},{3,2},{4,5},{5,4},{6,7},{7,6},{8,9},{9,8},{10,11... | collective-permute-start | bytes 24584 | tf_op jit(solution)/shard_map/ppermute | solution.py:44
  417.4 7.0 %collective-permute-start.3 = (f32[2048]{0:T(1024)S(1)}, f32[2048]{0:T(1024)S(1)}, u32[]{:S(2)}, u32[]{:S(2)}) collective-permute-start(f32[2048]{0:T(1024)S(1)} %add.124), channel_id=1, source_target_pairs={{0,2},{1,3},{2,0},{3,1},{4,6},{5,7},{6,4},{7,5},{8,10},{9,11},{10,... | collective-permute-start | bytes 24584 | tf_op jit(solution)/shard_map/ppermute | solution.py:44
Sparse Core Ops, SparseCore 0:
  9.5 69.3 all-gather.7
  81.9 65.2 all-gather.9
  150.3 85.8 all-gather.11
  294.5 71.2 all-gather.13
where the time goes:
time: 458 us; the launch traced here: 456 us
  waiting for transfers between devices  186 us (41%)
  blocking collectives  125 us (27%)
  local copies, waits for them, and re-layouts  48.5 us (11%)
  other arithmetic  41.3 us (9%)
  matrix products  26.4 us (6%)
  between operations  14.2 us (3%)
  starting transfers between devices  12.4 us (3%)
    all_gather x1, waiting for transfers between devices, on_device(): lax.all_gather(tokens, 'inner', axis=0, tiled=True)  85.3 us
    all_gather x1, waiting for transfers between devices, on_device(): full_cols = lax.all_gather(state_rows, 'inner', axis=2, tiled=True)  66.3 us
    unnamed x1, blocking collectives  42.4 us
    all_gather x1, blocking collectives, on_device(): lax.all_gather(state_weight, 'ctx', axis=0, tiled=True)  30.7 us
    dynamic_slice x60, local copies, waits for them, and re-layouts, one(): lax.dynamic_index_in_dim(a, turn, 0, False).astype(own.dtype)  29.4 us
    all_gather x1, blocking collectives, on_device(): lax.all_gather(step_weight, 'ctx', axis=0, tiled=True)  29.1 us
    all_to_all x1, blocking collectives, on_device(): lax.all_to_all(normed, 'inner', split_axis=0, concat_axis=1, tiled=True)  23.1 us
    all_gather x1, waiting for transfers between devices, entering(): lax.all_gather(a.astype(kind), axis)  22.2 us
  transfers between devices with their start and end apart: 8, of which 7 were waited for; matrix products, arithmetic and copies ran while one was open for 4% of the time, Pallas kernels for 0%

commit v1 on v0

--- a/solution.py
+++ b/solution.py
@@ -1,3 +1,4 @@
+import functools
 import jax
 import jax.numpy as jnp
 from jax import lax
@@ -10,6 +11,42 @@
 CONV = 4
 SPAN = 128
 EPSILON = 1e-05
+
+
+def obtain_tasks(raw, dim_i, bus_axis):
+    parts_out, local_part, piece_now = (
+        lax.psum(1, axis_name=bus_axis),
+        lax.axis_index(bus_axis),
+        raw.shape[dim_i],
+    )
+    blocks_here = [
+        hop_no * parts_out if u == dim_i else hop_no for u, hop_no in enumerate(raw.shape)
+    ]
+    val2 = jnp.zeros(blocks_here, raw.dtype)
+    p_next = lax.dynamic_update_slice_in_dim(val2, raw, local_part * piece_now, axis=dim_i)
+    prior = everything = raw
+    b = 1
+    while b < parts_out // 2 + 1:
+        prior = lax.ppermute(
+            prior, axis_name=bus_axis, perm=[(u, (u + 1) % parts_out) for u in range(parts_out)]
+        )
+        p_next = lax.dynamic_update_slice_in_dim(
+            p_next, prior, (local_part - b) % parts_out * piece_now, axis=dim_i
+        )
+        if 2 * b < parts_out:
+            everything = lax.ppermute(
+                everything,
+                axis_name=bus_axis,
+                perm=[(u, (u - 1) % parts_out) for u in range(parts_out)],
+            )
+            p_next = lax.dynamic_update_slice_in_dim(
+                p_next, everything, (local_part + b) % parts_out * piece_now, axis=dim_i
+            )
+        b = b + 1
+    return p_next
+
+
+edit_yards = functools.partial(obtain_tasks, dim_i=0, bus_axis="inner")
 
 
 def passed_along(x, axis, by):
@@ -100,11 +137,9 @@
         ],
         axis=1,
     )
-    projected = jnp.dot(
-        lax.all_gather(tokens, "inner", axis=0, tiled=True),
-        joined,
-        preferred_element_type=jnp.float32,
-    ).astype(jnp.bfloat16)
+    projected = jnp.dot(edit_yards(tokens), joined, preferred_element_type=jnp.float32).astype(
+        jnp.bfloat16
+    )
     rows_total = projected.shape[0]
     gate_values = projected[:, :width_here]
     x_pre = projected[:, width_here : 2 * width_here]

time: 458 us -> 442 us (0.965)
  waiting for transfers between devices: 186 us -> 83.5 us
  starting transfers between devices: 12.4 us -> 77.9 us
  local copies, waits for them, and re-layouts: 48.5 us -> 69.4 us
    all_gather x1 -> x0, waiting for transfers between devices: 85.3 us -> none  [on_device(): lax.all_gather(tokens, 'inner', axis=0, tiled=True)]
    all_gather x1, waiting for transfers between devices: 66.3 us -> 0.01 us  [on_device(): full_cols = lax.all_gather(state_rows, 'inner', axis=2, tiled=True)]
    ppermute x0 -> x15, starting transfers between devices: none -> 65.6 us  [the longest x7 48.8 us: obtain_tasks(): lax.ppermute(everything, axis_name=bus_axis, perm=[(u, (u - 1) % parts_ou...]
    ppermute x0 -> x15, waiting for transfers between devices: none -> 58.6 us  [the longest x7 30.4 us: obtain_tasks(): lax.ppermute(everything, axis_name=bus_axis, perm=[(u, (u - 1) % parts_ou...]
    dynamic_update_slice x0 -> x16, local copies, waits for them, and re-layouts: none -> 16.7 us  [the longest x8 8.89 us: obtain_tasks(): lax.dynamic_update_slice_in_dim(p_next, prior, (local_part - b) % parts_o...]
    all_gather x1, waiting for transfers between devices: 6.12 us -> 0.01 us  [on_device(): lax.all_gather(project_weight, 'ctx', axis=0, tiled=True)]
  transfers between devices with their start and end apart: 8 -> 22, of which waited for: 7 -> 12; matrix products, arithmetic and copies ran while one was open for 4% -> 8% of each run, Pallas kernels for 0% -> 0%
where the time goes in v1:
time: 442 us; the launch traced here: 439 us
  blocking collectives  126 us (29%)
  waiting for transfers between devices  83.5 us (19%)
  starting transfers between devices  77.9 us (18%)
  local copies, waits for them, and re-layouts  69.4 us (16%)
  other arithmetic  41.3 us (9%)
  matrix products  25.3 us (6%)
  between operations  14.6 us (3%)
    ppermute x7, starting transfers between devices, obtain_tasks(): lax.ppermute(everything, axis_name=bus_axis, perm=[(u, (u - 1) % parts_ou...  48.8 us
    unnamed x1, blocking collectives  42.7 us
    all_gather x1, blocking collectives, on_device(): lax.all_gather(state_weight, 'ctx', axis=0, tiled=True)  30.7 us
    ppermute x7, waiting for transfers between devices, obtain_tasks(): lax.ppermute(everything, axis_name=bus_axis, perm=[(u, (u - 1) % parts_ou...  30.4 us
    dynamic_slice x60, local copies, waits for them, and re-layouts, one(): lax.dynamic_index_in_dim(a, turn, 0, False).astype(own.dtype)  29.4 us
    all_gather x1, blocking collectives, on_device(): lax.all_gather(step_weight, 'ctx', axis=0, tiled=True)  29.1 us
    ppermute x8, waiting for transfers between devices, obtain_tasks(): lax.ppermute(prior, axis_name=bus_axis, perm=[(u, (u + 1) % parts_out) fo...  28.1 us
    all_to_all x1, blocking collectives, on_device(): lax.all_to_all(normed, 'inner', split_axis=0, concat_axis=1, tiled=True)  23.1 us
  transfers between devices with their start and end apart: 22, of which 12 were waited for; matrix products, arithmetic and copies ran while one was open for 8% of the time, Pallas kernels for 0%

profile of v1, /device:TPU:480, one launch (start us, length us, event | category | flops | bytes accessed | tf_op | source)
XLA Modules:
  0.0 439.1 jit_solution(16131535753167016374)
XLA Ops:
  8.1 30.7 %all_gather.23 = bf16[2048,2,32]{2,1,0:T(2,128)(2,1)S(1)} all-gather(bf16[64,2,32]{2,1,0:T(2,128)(2,1)S(1)} %copy.91), channel_id=1, replica_groups=mesh['ctx'=32,'inner'=16] {'ctx'}, dimensions={0}, use_global_device_ids=true | all-gather | bytes 270336 | tf_op jit(solution)/shard_map/all_gather | solution.py:121
  40.7 3.3 collective-permute-start
  44.0 5.8 %collective-permute-start.1 = (bf16[128,2048]{1,0:T(8,128)(2,1)S(1)}, bf16[128,2048]{1,0:T(8,128)(2,1)S(1)}, u32[]{:S(2)}, u32[]{:S(2)}) collective-permute-start(bf16[128,2048]{1,0:T(8,128)(2,1)S(1)} %copy-done.3), channel_id=1, source_target_pairs={{0,15},{1,0},{2,1},{3,2},{4,3},{5,4},{6,5},{7,6},{8,7},{9,8},{10,9... | collective-permute-start | bytes 1572872 | tf_op jit(solution)/shard_map/ppermute | solution.py:37
  49.8 10.2 %collective-permute-done = bf16[128,2048]{1,0:T(8,128)(2,1)S(1)} collective-permute-done((bf16[128,2048]{1,0:T(8,128)(2,1)S(1)}, bf16[128,2048]{1,0:T(8,128)(2,1)S(1)}, u32[]{:S(2)}, u32[]{:S(2)}) %collective-permute-start) | collective-permute-done | bytes 524320 | tf_op jit(solution)/shard_map/ppermute | solution.py:30
  60.0 1.9 collective-permute-start.2
  62.0 7.2 %collective-permute-start.3 = (bf16[128,2048]{1,0:T(8,128)(2,1)S(1)}, bf16[128,2048]{1,0:T(8,128)(2,1)S(1)}, u32[]{:S(2)}, u32[]{:S(2)}) collective-permute-start(bf16[128,2048]{1,0:T(8,128)(2,1)S(1)} %collective-permute-done.1), channel_id=1, source_target_pairs={{0,15},{1,0},{2,1},{3,2},{4,3},{5,4},{6,5},{7,6},{8,7},{9,8},{10,9... | collective-permute-start | bytes 1572872 | tf_op jit(solution)/shard_map/ppermute | solution.py:37
  69.2 9.4 %collective-permute-done.2 = bf16[128,2048]{1,0:T(8,128)(2,1)S(1)} collective-permute-done((bf16[128,2048]{1,0:T(8,128)(2,1)S(1)}, bf16[128,2048]{1,0:T(8,128)(2,1)S(1)}, u32[]{:S(2)}, u32[]{:S(2)}) %collective-permute-start.2) | collective-permute-done | bytes 524320 | tf_op jit(solution)/shard_map/ppermute | solution.py:30
  78.6 1.9 collective-permute-start.4
  80.6 4.3 broadcast_in_dim.28
  85.7 7.4 %collective-permute-start.5 = (bf16[128,2048]{1,0:T(8,128)(2,1)S(1)}, bf16[128,2048]{1,0:T(8,128)(2,1)}, u32[]{:S(2)}, u32[]{:S(2)}) collective-permute-start(bf16[128,2048]{1,0:T(8,128)(2,1)S(1)} %collective-permute-done.3), channel_id=1, source_target_pairs={{0,15},{1,0},{2,1},{3,2},{4,3},{5,4},{6,5},{7,6},{8,7},{9,8},{10,9... | collective-permute-start | bytes 1572872 | tf_op jit(solution)/shard_map/ppermute | solution.py:37
  93.2 3.1 collective-permute-done.4
  96.3 1.9 collective-permute-start.6
  98.5 29.1 %all-gather.2 = bf16[32,64,4]{1,2,0:T(4,128)(2,1)S(1)} all-gather(bf16[1,64,4]{1,2,0:T(4,128)(2,1)S(1)} %bitcast.100), channel_id=1, replica_groups=mesh['ctx'=32,'inner'=16] {'ctx'}, dimensions={0}, use_global_device_ids=true | all-gather | bytes 16896 | tf_op jit(solution)/shard_map/all_gather | solution.py:122
  129.9 1.9 constant_dynamic-update-slice_fusion.14
  131.9 7.2 %collective-permute-start.7 = (bf16[128,2048]{1,0:T(8,128)(2,1)}, bf16[128,2048]{1,0:T(8,128)(2,1)S(1)}, u32[]{:S(2)}, u32[]{:S(2)}) collective-permute-start(bf16[128,2048]{1,0:T(8,128)(2,1)} %collective-permute-done.5), channel_id=1, source_target_pairs={{0,15},{1,0},{2,1},{3,2},{4,3},{5,4},{6,5},{7,6},{8,7},{9,8},{10,9... | collective-permute-start | bytes 1572872 | tf_op jit(solution)/shard_map/ppermute | solution.py:37
  139.9 1.9 collective-permute-start.8
  143.6 15.0 %collective-permute-done.7 = bf16[128,2048]{1,0:T(8,128)(2,1)S(1)} collective-permute-done((bf16[128,2048]{1,0:T(8,128)(2,1)}, bf16[128,2048]{1,0:T(8,128)(2,1)S(1)}, u32[]{:S(2)}, u32[]{:S(2)}) %collective-permute-start.7) | collective-permute-done | bytes 524320 | tf_op jit(solution)/shard_map/ppermute | solution.py:37
  158.6 5.8 %collective-permute-start.9 = (bf16[128,2048]{1,0:T(8,128)(2,1)S(1)}, bf16[128,2048]{1,0:T(8,128)(2,1)S(1)}, u32[]{:S(2)}, u32[]{:S(2)}) collective-permute-start(bf16[128,2048]{1,0:T(8,128)(2,1)S(1)} %collective-permute-done.7), channel_id=1, source_target_pairs={{0,15},{1,0},{2,1},{3,2},{4,3},{5,4},{6,5},{7,6},{8,7},{9,8},{10,9... | collective-permute-start | bytes 1572872 | tf_op jit(solution)/shard_map/ppermute | solution.py:37
  165.2 1.9 collective-permute-start.10
  167.1 1.9 constant_dynamic-update-slice_fusion.9
  170.9 4.6 %collective-permute-done.9 = bf16[128,2048]{1,0:T(8,128)(2,1)S(1)} collective-permute-done((bf16[128,2048]{1,0:T(8,128)(2,1)S(1)}, bf16[128,2048]{1,0:T(8,128)(2,1)S(1)}, u32[]{:S(2)}, u32[]{:S(2)}) %collective-permute-start.9) | collective-permute-done | bytes 524320 | tf_op jit(solution)/shard_map/ppermute | solution.py:37
  175.5 7.7 %collective-permute-start.11 = (bf16[128,2048]{1,0:T(8,128)(2,1)S(1)}, bf16[128,2048]{1,0:T(8,128)(2,1)S(1)}, u32[]{:S(2)}, u32[]{:S(2)}) collective-permute-start(bf16[128,2048]{1,0:T(8,128)(2,1)S(1)} %collective-permute-done.9), channel_id=1, source_target_pairs={{0,15},{1,0},{2,1},{3,2},{4,3},{5,4},{6,5},{7,6},{8,7},{9,8},{10,9... | collective-permute-start | bytes 1572872 | tf_op jit(solution)/shard_map/ppermute | solution.py:37
  184.1 1.9 collective-permute-start.12
  187.7 5.9 %collective-permute-done.11 = bf16[128,2048]{1,0:T(8,128)(2,1)S(1)} collective-permute-done((bf16[128,2048]{1,0:T(8,128)(2,1)S(1)}, bf16[128,2048]{1,0:T(8,128)(2,1)S(1)}, u32[]{:S(2)}, u32[]{:S(2)}) %collective-permute-start.11) | collective-permute-done | bytes 524320 | tf_op jit(solution)/shard_map/ppermute | solution.py:37
  193.6 7.7 %collective-permute-start.13 = (bf16[128,2048]{1,0:T(8,128)(2,1)S(1)}, bf16[128,2048]{1,0:T(8,128)(2,1)S(1)}, u32[]{:S(2)}, u32[]{:S(2)}) collective-permute-start(bf16[128,2048]{1,0:T(8,128)(2,1)S(1)} %collective-permute-done.11), channel_id=1, source_target_pairs={{0,15},{1,0},{2,1},{3,2},{4,3},{5,4},{6,5},{7,6},{8,7},{9,8},{10,9... | collective-permute-start | bytes 1572872 | tf_op jit(solution)/shard_map/ppermute | solution.py:37
  202.1 1.9 collective-permute-start.14
  205.7 4.9 %collective-permute-done.13 = bf16[128,2048]{1,0:T(8,128)(2,1)S(1)} collective-permute-done((bf16[128,2048]{1,0:T(8,128)(2,1)S(1)}, bf16[128,2048]{1,0:T(8,128)(2,1)S(1)}, u32[]{:S(2)}, u32[]{:S(2)}) %collective-permute-start.13) | collective-permute-done | bytes 524320 | tf_op jit(solution)/shard_map/ppermute | solution.py:37
  211.5 2.0 copy.123
  213.5 5.4 %collective-permute-done.14 = bf16[128,2048]{1,0:T(8,128)(2,1)S(1)} collective-permute-done((bf16[128,2048]{1,0:T(8,128)(2,1)S(1)}, bf16[128,2048]{1,0:T(8,128)(2,1)S(1)}, u32[]{:S(2)}, u32[]{:S(2)}) %collective-permute-start.14) | collective-permute-done | bytes 524320 | tf_op jit(solution)/shard_map/ppermute | solution.py:30
  219.8 1.9 constant_dynamic-slice_fusion.2
  223.4 9.7 %fusion.9 = bf16[2048,772]{0,1:T(8,128)(2,1)S(1)} fusion(bf16[2048,2048]{1,0:T(8,128)(2,1)} %constant_dynamic-update-slice_fusion, bf16[2048,4]{1,0:T(8,128)(2,1)} %bitcast.90, bf16[2048,256]{1,0:T(8,128)(2,1)} %copy.95, bf16[2048,512]{1,0:T(8,128)(2,1)S(1)} %bitcast.89), kind=kOutput, calls=%fused_computation.20 | convolution fusion | flops 6487072768 | bytes 14712832 | tf_op jit(solution)/shard_map/dot_general | solution.py:140
  236.3 1.9 collective-permute-start.15
  238.3 2.1 collective-permute-start.16
  241.9 2.2 fusion.48
  244.3 2.2 multiply_convert_fusion.7
  247.0 4.0 fusion.23
  250.9 28.8 %while.26 = (s32[]{:T(128)}, f32[4,128,64]{2,1,0:T(8,128)S(1)}, f32[16,4,128,64]{3,2,1,0:T(8,128)}, f32[16,4]{1,0:T(8,128)S(1)}, f32[16,4,128,64]{3,2,1,0:T(8,128)}, /*index=5*/s32[]{:T(128)}, s32[]{:T(128)}) while((s32[]{:T(128)}, f32[4,128,64]{2,1,0:T(8,128)S(1)}, f32[16,4,128,64]{3,2,1,0:T(8,128)}, f32[16,4]{1,0:T(8,128)S(1)}, ...), condition=%wide.region_2.3_spmd.clone, body=%wide.region_1.2_spmd.clone.sunk | while | flops 131075 | bytes 787088 | solution.py:171
  282.9 42.7 %all-reduce = bf16[128]{0:T(256)(128)(2,1)S(1)} all-reduce(bf16[128]{0:T(256)(128)(2,1)S(1)} %dynamic-update-slice), channel_id=2, replica_groups=mesh['ctx'=32,'inner'=16] {'ctx'}, use_global_device_ids=true, to_apply=%add | all-reduce | flops 128 | bytes 512
  326.6 3.3 fusion.15
  329.9 19.3 %all-gather.11.cloned.1.call-done = bf16[128,128,64]{1,2,0:T(8,128)(2,1)} async-done(((bf16[4,128,64]{1,2,0:T(8,128)(2,1)}), bf16[128,128,64]{1,2,0:T(8,128)(2,1)}) %all-gather.11.cloned.1.call-update) | async-done | bytes 2097168 | tf_op jit(solution)/shard_map/all_gather | solution.py:61
  349.2 34.4 %while.25 = (s32[]{:T(128)}, f32[4,128,64]{2,1,0:T(8,128)S(1)}, s32[]{:T(128)}, bf16[32,4]{1,0:T(8,128)(2,1)S(1)}, bf16[32,4,128,64]{2,3,1,0:T(8,128)(2,1)}, /*index=5*/s32[]{:T(128)}, s32[]{:T(128)}, s32[]{:T(128)}) while((s32[]{:T(128)}, f32[4,128,64]{2,1,0:T(8,128)S(1)}, s32[]{:T(128)}, bf16[32,4]{1,0:T(8,128)(2,1)S(1)}, ...), condition=%wide.region_6.7_spmd, body=%wide.region_5.6_spmd.sunk | while | flops 98313 | bytes 589991 | solution.py:75
  383.6 5.2 %fusion.12 = f32[16,4,64,128]{3,2,1,0:T(8,128)S(1)} fusion(f32[16,4,128,64]{3,2,1,0:T(8,128)} %get-tuple-element.77, f32[4,16,128]{2,0,1:T(4,128)S(1)} %copy.110, f32[16,128,128]{2,1,0:T(8,128)S(1)} %convert_element_type.131, f32[4,128,64]{2,1,0:T(8,128)S(1)} %get-tuple-element.79, f32[16,4]{1,0:T(8,128)S(1)} %copy.107), kind=kOutput, calls=%fused_computation.21 | convolution fusion | flops 139460608 | bytes 5406976 | tf_op jit(solution)/shard_map/hctn,chnp->cthp/dot_general | solution.py:184
  388.8 2.7 add_bitcast_fusion
  392.8 2.4 fusion.20
  395.2 3.4 collective-permute-start.17
  398.5 2.2 collective-permute-done.17
  400.7 4.9 %collective-permute-start.18 = (f32[2048]{0:T(1024)S(1)}, f32[2048]{0:T(1024)S(1)}, u32[]{:S(2)}, u32[]{:S(2)}) collective-permute-start(f32[2048]{0:T(1024)S(1)} %add.285), channel_id=1, source_target_pairs={{0,2},{1,3},{2,0},{3,1},{4,6},{5,7},{6,4},{7,5},{8,10},{9,11},{10,... | collective-permute-start | bytes 24584 | tf_op jit(solution)/shard_map/ppermute | solution.py:81
  408.2 23.1 %all_to_all.19 = bf16[16,128,256]{1,2,0:T(8,128)(2,1)S(1)} all-to-all(bf16[16,128,256]{1,2,0:T(8,128)(2,1)S(1)} %copy_bitcast_fusion), channel_id=1, replica_groups=mesh['ctx'=32,'inner'=16] {'inner'}, dimensions={0} | all-to-all | bytes 2097152 | tf_op jit(solution)/shard_map/all_to_all | solution.py:197
  (269 shorter events, 95.9 us)
Async XLA Ops:
  6.5 34.1 %copy-start.3 = (bf16[128,2048]{1,0:T(8,128)(2,1)S(1)}, bf16[128,2048]{1,0:T(8,128)(2,1)}, u32[]{:S(2)}) copy-start(bf16[128,2048]{1,0:T(8,128)(2,1)} %param.13) | copy-start | bytes 1572868
  6.5 204.9 %all-gather.7.cloned.1.call-start = ((), (), s32[]{:S(2)}) async-start(), calls=%async_computation.1 | async-start | bytes 2162688 | tf_op jit(solution)/shard_map/all_gather | solution.py:120
  7.3 212.5 %all-gather.9.cloned.1.call-start = ((), (), s32[]{:S(2)}) async-start(), calls=%async_computation.2 | async-start | bytes 4456448 | tf_op jit(solution)/shard_map/all_gather | solution.py:128
  40.6 308.6 %all-gather.11.cloned.1.call-start = ((), (), s32[]{:S(2)}) async-start(), calls=%async_computation.3 | async-start | bytes 2162688 | tf_op jit(solution)/shard_map/all_gather | solution.py:61
  40.7 19.4 %collective-permute-start = (bf16[128,2048]{1,0:T(8,128)(2,1)S(1)}, bf16[128,2048]{1,0:T(8,128)(2,1)S(1)}, u32[]{:S(2)}, u32[]{:S(2)}) collective-permute-start(bf16[128,2048]{1,0:T(8,128)(2,1)S(1)} %copy-done.3), channel_id=1, source_target_pairs={{0,1},{1,2},{2,3},{3,4},{4,5},{5,6},{6,7},{7,8},{8,9},{9,10},{10,1... | collective-permute-start | bytes 1572872 | tf_op jit(solution)/shard_map/ppermute | solution.py:30
  44.0 18.0 %collective-permute-start.1 = (bf16[128,2048]{1,0:T(8,128)(2,1)S(1)}, bf16[128,2048]{1,0:T(8,128)(2,1)S(1)}, u32[]{:S(2)}, u32[]{:S(2)}) collective-permute-start(bf16[128,2048]{1,0:T(8,128)(2,1)S(1)} %copy-done.3), channel_id=1, source_target_pairs={{0,15},{1,0},{2,1},{3,2},{4,3},{5,4},{6,5},{7,6},{8,7},{9,8},{10,9... | collective-permute-start | bytes 1572872 | tf_op jit(solution)/shard_map/ppermute | solution.py:37
  60.0 24.8 %copy-start.6 = (bf16[128,2048]{1,0:T(8,128)(2,1)}, bf16[128,2048]{1,0:T(8,128)(2,1)S(1)}, u32[]{:S(2)}) copy-start(bf16[128,2048]{1,0:T(8,128)(2,1)S(1)} %collective-permute-done) | copy-start | bytes 1572868
  60.0 18.6 %collective-permute-start.2 = (bf16[128,2048]{1,0:T(8,128)(2,1)S(1)}, bf16[128,2048]{1,0:T(8,128)(2,1)S(1)}, u32[]{:S(2)}, u32[]{:S(2)}) collective-permute-start(bf16[128,2048]{1,0:T(8,128)(2,1)S(1)} %collective-permute-done), channel_id=1, source_target_pairs={{0,1},{1,2},{2,3},{3,4},{4,5},{5,6},{6,7},{7,8},{8,9},{9,10},{10,1... | collective-permute-start | bytes 1572872 | tf_op jit(solution)/shard_map/ppermute | solution.py:30
  62.0 22.9 %copy-start.4 = (bf16[128,2048]{1,0:T(8,128)(2,1)}, bf16[128,2048]{1,0:T(8,128)(2,1)S(1)}, u32[]{:S(2)}) copy-start(bf16[128,2048]{1,0:T(8,128)(2,1)S(1)} %collective-permute-done.1) | copy-start | bytes 1572868
  62.0 23.8 %collective-permute-start.3 = (bf16[128,2048]{1,0:T(8,128)(2,1)S(1)}, bf16[128,2048]{1,0:T(8,128)(2,1)S(1)}, u32[]{:S(2)}, u32[]{:S(2)}) collective-permute-start(bf16[128,2048]{1,0:T(8,128)(2,1)S(1)} %collective-permute-done.1), channel_id=1, source_target_pairs={{0,15},{1,0},{2,1},{3,2},{4,3},{5,4},{6,5},{7,6},{8,7},{9,8},{10,9... | collective-permute-start | bytes 1572872 | tf_op jit(solution)/shard_map/ppermute | solution.py:37
  78.6 17.7 %collective-permute-start.4 = (bf16[128,2048]{1,0:T(8,128)(2,1)S(1)}, bf16[128,2048]{1,0:T(8,128)(2,1)S(1)}, u32[]{:S(2)}, u32[]{:S(2)}) collective-permute-start(bf16[128,2048]{1,0:T(8,128)(2,1)S(1)} %collective-permute-done.2), channel_id=1, source_target_pairs={{0,1},{1,2},{2,3},{3,4},{4,5},{5,6},{6,7},{7,8},{8,9},{9,10},{10,1... | collective-permute-start | bytes 1572872 | tf_op jit(solution)/shard_map/ppermute | solution.py:30
  80.5 12.6 %copy-start.8 = (f32[5,256]{1,0:T(8,128)S(1)}, f32[5,256]{1,0:T(8,128)}, u32[]{:S(2)}) copy-start(f32[5,256]{1,0:T(8,128)} %param.17) | copy-start | bytes 15364
  80.6 17.7 %copy-start.11 = (f32[4]{0:T(128)S(1)}, f32[4]{0:T(128)}, u32[]{:S(2)}) copy-start(f32[4]{0:T(128)} %param.20) | copy-start | bytes 52
  80.6 17.9 %copy-start.9 = (bf16[64,4]{0,1:T(4,128)(2,1)S(1)}, bf16[64,4]{0,1:T(4,128)(2,1)}, u32[]{:S(2)}) copy-start(bf16[64,4]{0,1:T(4,128)(2,1)} %param.16) | copy-start | bytes 1540
  84.9 43.8 %copy-start.7 = (f32[5,2,512]{2,1,0:T(2,128)S(1)}, f32[5,2,512]{2,1,0:T(2,128)}, u32[]{:S(2)}) copy-start(f32[5,2,512]{2,1,0:T(2,128)} %param.18) | copy-start | bytes 61444
  85.7 53.4 %copy-start.5 = (bf16[128,2048]{1,0:T(8,128)(2,1)S(1)}, bf16[128,2048]{1,0:T(8,128)(2,1)}, u32[]{:S(2)}) copy-start(bf16[128,2048]{1,0:T(8,128)(2,1)} %copy-done.4) | copy-start | bytes 1572868
  85.7 46.1 %collective-permute-start.5 = (bf16[128,2048]{1,0:T(8,128)(2,1)S(1)}, bf16[128,2048]{1,0:T(8,128)(2,1)}, u32[]{:S(2)}, u32[]{:S(2)}) collective-permute-start(bf16[128,2048]{1,0:T(8,128)(2,1)S(1)} %collective-permute-done.3), channel_id=1, source_target_pairs={{0,15},{1,0},{2,1},{3,2},{4,3},{5,4},{6,5},{7,6},{8,7},{9,8},{10,9... | collective-permute-start | bytes 1572872 | tf_op jit(solution)/shard_map/ppermute | solution.py:37
  96.3 43.7 %collective-permute-start.6 = (bf16[128,2048]{1,0:T(8,128)(2,1)S(1)}, bf16[128,2048]{1,0:T(8,128)(2,1)}, u32[]{:S(2)}, u32[]{:S(2)}) collective-permute-start(bf16[128,2048]{1,0:T(8,128)(2,1)S(1)} %collective-permute-done.4), channel_id=1, source_target_pairs={{0,1},{1,2},{2,3},{3,4},{4,5},{5,6},{6,7},{7,8},{8,9},{9,10},{10,1... | collective-permute-start | bytes 1572872 | tf_op jit(solution)/shard_map/ppermute | solution.py:30
  131.9 26.7 %collective-permute-start.7 = (bf16[128,2048]{1,0:T(8,128)(2,1)}, bf16[128,2048]{1,0:T(8,128)(2,1)S(1)}, u32[]{:S(2)}, u32[]{:S(2)}) collective-permute-start(bf16[128,2048]{1,0:T(8,128)(2,1)} %collective-permute-done.5), channel_id=1, source_target_pairs={{0,15},{1,0},{2,1},{3,2},{4,3},{5,4},{6,5},{7,6},{8,7},{9,8},{10,9... | collective-permute-start | bytes 1572872 | tf_op jit(solution)/shard_map/ppermute | solution.py:37
  139.9 25.3 %collective-permute-start.8 = (bf16[128,2048]{1,0:T(8,128)(2,1)}, bf16[128,2048]{1,0:T(8,128)(2,1)S(1)}, u32[]{:S(2)}, u32[]{:S(2)}) collective-permute-start(bf16[128,2048]{1,0:T(8,128)(2,1)} %collective-permute-done.6), channel_id=1, source_target_pairs={{0,1},{1,2},{2,3},{3,4},{4,5},{5,6},{6,7},{7,8},{8,9},{9,10},{10,1... | collective-permute-start | bytes 1572872 | tf_op jit(solution)/shard_map/ppermute | solution.py:30
  158.6 17.0 %collective-permute-start.9 = (bf16[128,2048]{1,0:T(8,128)(2,1)S(1)}, bf16[128,2048]{1,0:T(8,128)(2,1)S(1)}, u32[]{:S(2)}, u32[]{:S(2)}) collective-permute-start(bf16[128,2048]{1,0:T(8,128)(2,1)S(1)} %collective-permute-done.7), channel_id=1, source_target_pairs={{0,15},{1,0},{2,1},{3,2},{4,3},{5,4},{6,5},{7,6},{8,7},{9,8},{10,9... | collective-permute-start | bytes 1572872 | tf_op jit(solution)/shard_map/ppermute | solution.py:37
  165.2 18.9 %collective-permute-start.10 = (bf16[128,2048]{1,0:T(8,128)(2,1)S(1)}, bf16[128,2048]{1,0:T(8,128)(2,1)S(1)}, u32[]{:S(2)}, u32[]{:S(2)}) collective-permute-start(bf16[128,2048]{1,0:T(8,128)(2,1)S(1)} %collective-permute-done.8), channel_id=1, source_target_pairs={{0,1},{1,2},{2,3},{3,4},{4,5},{5,6},{6,7},{7,8},{8,9},{9,10},{10,1... | collective-permute-start | bytes 1572872 | tf_op jit(solution)/shard_map/ppermute | solution.py:30
  175.5 18.0 %collective-permute-start.11 = (bf16[128,2048]{1,0:T(8,128)(2,1)S(1)}, bf16[128,2048]{1,0:T(8,128)(2,1)S(1)}, u32[]{:S(2)}, u32[]{:S(2)}) collective-permute-start(bf16[128,2048]{1,0:T(8,128)(2,1)S(1)} %collective-permute-done.9), channel_id=1, source_target_pairs={{0,15},{1,0},{2,1},{3,2},{4,3},{5,4},{6,5},{7,6},{8,7},{9,8},{10,9... | collective-permute-start | bytes 1572872 | tf_op jit(solution)/shard_map/ppermute | solution.py:37
  184.1 18.0 %collective-permute-start.12 = (bf16[128,2048]{1,0:T(8,128)(2,1)S(1)}, bf16[128,2048]{1,0:T(8,128)(2,1)S(1)}, u32[]{:S(2)}, u32[]{:S(2)}) collective-permute-start(bf16[128,2048]{1,0:T(8,128)(2,1)S(1)} %collective-permute-done.10), channel_id=1, source_target_pairs={{0,1},{1,2},{2,3},{3,4},{4,5},{5,6},{6,7},{7,8},{8,9},{9,10},{10,1... | collective-permute-start | bytes 1572872 | tf_op jit(solution)/shard_map/ppermute | solution.py:30
  193.6 17.1 %collective-permute-start.13 = (bf16[128,2048]{1,0:T(8,128)(2,1)S(1)}, bf16[128,2048]{1,0:T(8,128)(2,1)S(1)}, u32[]{:S(2)}, u32[]{:S(2)}) collective-permute-start(bf16[128,2048]{1,0:T(8,128)(2,1)S(1)} %collective-permute-done.11), channel_id=1, source_target_pairs={{0,15},{1,0},{2,1},{3,2},{4,3},{5,4},{6,5},{7,6},{8,7},{9,8},{10,9... | collective-permute-start | bytes 1572872 | tf_op jit(solution)/shard_map/ppermute | solution.py:37
  202.1 16.8 %collective-permute-start.14 = (bf16[128,2048]{1,0:T(8,128)(2,1)S(1)}, bf16[128,2048]{1,0:T(8,128)(2,1)S(1)}, u32[]{:S(2)}, u32[]{:S(2)}) collective-permute-start(bf16[128,2048]{1,0:T(8,128)(2,1)S(1)} %collective-permute-done.12), channel_id=1, source_target_pairs={{0,1},{1,2},{2,3},{3,4},{4,5},{5,6},{6,7},{7,8},{8,9},{9,10},{10,1... | collective-permute-start | bytes 1572872 | tf_op jit(solution)/shard_map/ppermute | solution.py:30
  233.1 1.7 copy-start.1
  233.1 1.7 copy-start.10
  236.3 5.6 %collective-permute-start.15 = (bf16[3,256]{0,1:T(8,128)(2,1)S(1)}, bf16[3,256]{0,1:T(8,128)(2,1)S(1)}, u32[]{:S(2)}, u32[]{:S(2)}) collective-permute-start(bf16[3,256]{0,1:T(8,128)(2,1)S(1)} %get-tuple-element.164), channel_id=1, source_target_pairs={{0,16},{16,32},{32,48},{48,64},{64,80},{80,96},{96,112},{112,128},... | collective-permute-start | bytes 4616 | tf_op jit(solution)/shard_map/ppermute | solution.py:55
  238.3 5.9 %collective-permute-start.16 = (bf16[3,2,128]{0,2,1:T(8,128)(2,1)S(1)}, bf16[3,2,128]{0,2,1:T(8,128)(2,1)S(1)}, u32[]{:S(2)}, u32[]{:S(2)}) collective-permute-start(bf16[3,2,128]{0,2,1:T(8,128)(2,1)S(1)} %bitcast.92), channel_id=1, source_target_pairs={{0,16},{16,32},{32,48},{48,64},{64,80},{80,96},{96,112},{112,128},... | collective-permute-start | bytes 4616 | tf_op jit(solution)/shard_map/ppermute | solution.py:55
  383.6 5.2 %copy-start = (f32[16,4,128,64]{3,2,1,0:T(8,128)S(1)}, f32[16,4,128,64]{3,2,1,0:T(8,128)}, u32[]{:S(2)}) copy-start(f32[16,4,128,64]{3,2,1,0:T(8,128)} %get-tuple-element.77) | copy-start | bytes 6291460
  383.6 5.2 %copy-start.2 = (f32[16,4,64,128]{3,2,1,0:T(8,128)S(1)}, f32[16,4,64,128]{3,2,1,0:T(8,128)}, u32[]{:S(2)}) copy-start(f32[16,4,64,128]{3,2,1,0:T(8,128)} %fusion.15) | copy-start | bytes 6291460
  395.2 5.5 %collective-permute-start.17 = (f32[2048]{0:T(1024)S(1)}, f32[2048]{0:T(1024)S(1)}, u32[]{:S(2)}, u32[]{:S(2)}) collective-permute-start(f32[2048]{0:T(1024)S(1)} %get-tuple-element.160), channel_id=1, source_target_pairs={{0,1},{1,0},{2,3},{3,2},{4,5},{5,4},{6,7},{7,6},{8,9},{9,8},{10,11... | collective-permute-start | bytes 24584 | tf_op jit(solution)/shard_map/ppermute | solution.py:81
  400.7 7.0 %collective-permute-start.18 = (f32[2048]{0:T(1024)S(1)}, f32[2048]{0:T(1024)S(1)}, u32[]{:S(2)}, u32[]{:S(2)}) collective-permute-start(f32[2048]{0:T(1024)S(1)} %add.285), channel_id=1, source_target_pairs={{0,2},{1,3},{2,0},{3,1},{4,6},{5,7},{6,4},{7,5},{8,10},{9,11},{10,... | collective-permute-start | bytes 24584 | tf_op jit(solution)/shard_map/ppermute | solution.py:81
Sparse Core Ops, SparseCore 0:
  9.5 69.4 all-gather.6
  82.0 81.0 all-gather.8
  280.6 68.4 all-gather.10
